TPU v7x, 512 devices: a whole 4x8x8 slice. The times are simulated.
512 devices in a mesh: dp: 64 (over z, x, core), mp: 8 (over y).
Axes of the slice: x: 4, y: 8, z: 8, core: 2. Of those that a mesh axis runs over, the one named last changes fastest.
Arguments:
- teacher_in: bfloat16 [64, 1024, 1408], P('dp', 'mp'), may hold values from -8 to 8
- teacher_gain: float32 [1408], replicated, may hold values from 0.5 to 1.5
- teacher_qkv: bfloat16 [3, 1408, 1408], P(None, 'mp'), may hold values from -1 to 1
- teacher_out: bfloat16 [1408, 1408], P('mp'), may hold values from -0.15625 to 0.15625
- student_in: bfloat16 [64, 1024, 1024], P('dp', None, 'mp'), may hold values from -6 to 6
- student_gain: float32 [1024], replicated, may hold values from 0.25 to 1.75
- widen_weight: bfloat16 [1024, 4096], P(None, 'mp'), may hold values from -0.1875 to 0.1875
- narrow_weight: bfloat16 [4096, 1024], P('mp'), may hold values from -0.09375 to 0.09375
- target_head: bfloat16 [1408, 1024], P('mp'), may hold values from -0.1875 to 0.1875
- positions: int32 [64, 512], P('dp'), may hold values from 0 to 1023, as said below
- counts: int32 [64], P('dp'), may hold values from 1 to 512, 16384 in all
Outputs:
- grad_widen: float32 [1024, 4096], P('dp', 'mp')
- grad_narrow: float32 [1024, 4096], P('dp', 'mp')
- losses: float32 [64], P('dp')
Inputs may be any that keep to these rules, and one draw needn't show every extreme that they name: `positions`: the entries of one image's list are distinct; only the first counts of them are live. The counts of all images sum to 16384.
All inputs are finite; a program needn't handle non-finite values. No bound on the sum of `counts` on one device may be relied on, other than what follows from the above.
Results may differ from a plain program's by a relative error of at most 0.02.
Values may be sent and summed in bfloat16 or wider, within the bound.
No kernel may reach another device: no remote copies, remote signals or barrier semaphores. Data moves between devices by JAX's collectives and lax.ppermute only.
A program may use at most 64 MiB of HBM per device.

v0:
```python
import jax
import jax.numpy as jnp
from jax import lax
from jax.sharding import Mesh, PartitionSpec as P

TD = 1408
TH = 16
EPSILON = 1e-06
DP = ("z", "x", "c")
BF = jnp.bfloat16
F32 = jnp.float32


def layer_norm(values, gain):
    mean_val = jnp.mean(values, axis=-1, keepdims=True)
    centred = values - mean_val
    spread = jnp.mean(centred * centred, axis=-1, keepdims=True)
    return centred * lax.rsqrt(spread + EPSILON) * gain


def gelu_value(pre):
    return 0.5 * pre * (1.0 + lax.erf(pre * 0.7071067811865476))


def gelu_slope(pre):
    return 0.5 * (1.0 + lax.erf(pre * 0.7071067811865476)) + pre * 0.3989422804014327 * jnp.exp(
        -0.5 * pre * pre
    )


def shift(amount):
    return [(i, (i + amount) % 8) for i in range(8)]


def ring(block):
    held = [block] + [None] * 7
    right = left = block
    for step in range(1, 5):
        right = lax.ppermute(right, "mp", shift(1))
        held[step] = right
        if step < 4:
            left = lax.ppermute(left, "mp", shift(-1))
            held[8 - step] = left
    return held


def reordered(stacked, me):
    return jnp.stack(
        [lax.dynamic_index_in_dim(stacked, (me - owner) % 8, 0, False) for owner in range(8)]
    )


def to_tiles(shard, per_piece):
    rows, cols = shard.shape
    tiles = shard.reshape(rows // 8, 8, cols // 128, 128).transpose(0, 2, 1, 3)
    tiles = tiles.reshape(-1, 8, 128)
    spare = 64 * per_piece - tiles.shape[0]
    tiles = jnp.concatenate([tiles, jnp.zeros((spare, 8, 128), tiles.dtype)])
    return tiles.reshape(64, per_piece, 8, 128)


def from_tiles(pieces, rows, cols):
    count = rows // 8 * (cols // 128)
    tiles = pieces[:, :count].reshape(8, rows // 8, cols // 128, 8, 128)
    return tiles.transpose(0, 1, 3, 2, 4).reshape(8 * rows, cols)


def on_device(
    teacher_in,
    teacher_gain,
    teacher_qkv,
    teacher_out,
    student_in,
    student_gain,
    widen_weight,
    narrow_weight,
    target_head,
    positions,
    counts,
):
    me = lax.axis_index("mp")
    at = lax.axis_index(DP)
    picked = positions[0]
    live_count = counts[0]
    head = TD // TH
    factor = head ** (-0.5)
    mine = jnp.concatenate(
        [
            lax.dynamic_index_in_dim(to_tiles(teacher_out, 4), at, 0, False),
            lax.dynamic_index_in_dim(to_tiles(target_head, 3), at, 0, False),
        ]
    )
    shares = lax.all_to_all(jnp.broadcast_to(mine, (8, *mine.shape)), "mp", 0, 0, tiled=True)
    out_full = from_tiles(lax.all_gather(shares[:, :4], DP, axis=1, tiled=True), 176, 1408)
    head_full = from_tiles(lax.all_gather(shares[:, 4:], DP, axis=1, tiled=True), 176, 1024)
    rows = student_in[0][picked]
    packed = jnp.concatenate([rows[128 * g : 128 * g + 128] for g in range(4)], axis=1)
    held = ring(jnp.concatenate([teacher_in[0], packed], axis=1))
    stacked = jnp.stack([h[:, TD:] for h in held])
    by_owner = reordered(stacked, me).reshape(8, 128, 4, 128)
    student = by_owner.transpose(2, 1, 0, 3).reshape(512, 1024)
    normed_rows = layer_norm(student.astype(F32), student_gain).astype(BF)
    pre_act = jnp.dot(normed_rows, widen_weight, preferred_element_type=F32)
    activity = gelu_value(pre_act).astype(BF)
    partial = jnp.dot(activity, narrow_weight, preferred_element_type=F32).astype(BF)
    arrived = lax.all_to_all(partial.reshape(8, 64, 1024), "mp", 0, 0, tiled=True)
    branch = jnp.sum(arrived.astype(F32), axis=0)
    own_rows = lax.dynamic_slice_in_dim(student, me * 64, 64, 0)
    outputs = (own_rows.astype(F32) + branch).astype(BF)
    weights = jnp.pad(
        teacher_qkv.reshape(3, 2, head, TD), ((0, 0), (0, 0), (0, 128 - head), (0, 0))
    )
    weights = weights.reshape(768, TD)
    made = []
    for h in held:
        normed = layer_norm(h[:, :TD].astype(F32), teacher_gain).astype(BF)
        made.append(jnp.einsum("pi,oi->po", normed, weights, preferred_element_type=F32).astype(BF))
    made = jnp.concatenate(made)
    place = (me - picked // 128) % 8 * 128 + picked % 128
    query = made[:, :256][place].reshape(512, 2, 128)
    key = made[:, 256:512].reshape(1024, 2, 128)
    value = made[:, 512:].reshape(1024, 2, 128)
    scores = jnp.einsum("shd,phd->hsp", query, key, preferred_element_type=F32) * factor
    soft_num = jnp.exp(scores - jnp.max(scores, axis=-1, keepdims=True))
    soft = (soft_num / jnp.sum(soft_num, axis=-1, keepdims=True)).astype(BF)
    attended = jnp.einsum("hsp,phd->shd", soft, value, preferred_element_type=F32)
    attended = attended[:, :, :head].astype(BF).reshape(8, 64, 176)
    attended = lax.all_to_all(attended, "mp", 0, 0, tiled=True)
    attended = attended.transpose(1, 0, 2).reshape(64, TD)
    own_place = lax.dynamic_slice_in_dim(place, me * 64, 64, 0)
    patches = jnp.concatenate([h[:, :TD] for h in held])
    blended = jnp.einsum("sw,ow->so", attended, out_full, preferred_element_type=F32)
    targets = (patches[own_place].astype(F32) + blended).astype(BF).astype(F32)
    slot = me * 64 + jnp.arange(64, dtype=jnp.int32)
    row_weight = jnp.where(slot < live_count, 1.0 / live_count.astype(F32), jnp.zeros((), F32))
    predicted = jnp.einsum("rd,cd->rc", outputs, head_full, preferred_element_type=F32)
    inner = jnp.sum(predicted * targets, axis=-1)
    inv_pred = lax.rsqrt(jnp.sum(predicted * predicted, axis=-1) + EPSILON)
    inv_target = lax.rsqrt(jnp.sum(targets * targets, axis=-1) + EPSILON)
    cosine = inner * inv_pred * inv_target
    row_loss = row_weight * (1.0 - cosine)
    slope = (row_weight * cosine * inv_pred * inv_pred)[:, None] * predicted - (
        row_weight * inv_pred * inv_target
    )[:, None] * targets
    back_own = jnp.dot(slope.astype(BF), head_full, preferred_element_type=F32).astype(BF)
    loss_high = row_loss.astype(BF)
    loss_low = (row_loss - loss_high.astype(F32)).astype(BF)
    extra = jnp.pad(jnp.stack([loss_high, loss_low], axis=1), ((0, 0), (0, 126)))
    back_held = jnp.stack(ring(jnp.concatenate([back_own, extra], axis=1)))
    back_held = reordered(back_held, me).reshape(512, 1152)
    image_loss = jnp.sum(back_held[:, 1024:].astype(F32))
    back = back_held[:, :1024]
    back_act = jnp.einsum("rd,hd->rh", back, narrow_weight, preferred_element_type=F32)
    back_pre = (back_act * gelu_slope(pre_act)).astype(BF)
    grad_w = jnp.einsum("rd,rh->dh", normed_rows, back_pre, preferred_element_type=F32)
    grad_n = jnp.einsum("rd,rh->dh", back, activity, preferred_element_type=F32)
    grads = jnp.concatenate(
        [grad_w.astype(BF).reshape(32, 2, 16, 512), grad_n.astype(BF).reshape(32, 2, 16, 512)], 2
    )
    core = lax.axis_index("c")
    other = lax.ppermute(lax.dynamic_index_in_dim(grads, 1 - core, 1, False), "c", [(0, 1), (1, 0)])
    kept = lax.dynamic_index_in_dim(grads, core, 1, False).astype(F32) + other.astype(F32)
    kept = kept.astype(BF).reshape(8, 4, 32, 512)
    kept = lax.all_to_all(kept, "x", 1, 0, tiled=False)
    kept = jnp.sum(kept.astype(F32), axis=0).astype(BF)
    kept = lax.all_to_all(kept, "z", 0, 0, tiled=True)
    total = jnp.sum(kept.astype(F32), axis=0)
    return (total[:16], total[16:], jnp.reshape(image_loss, (1,)))


def solution(mesh):
    grid = Mesh(mesh.devices.reshape(8, 4, 2, 8), ("z", "x", "c", "mp"))
    placed = (
        P(DP, "mp", None),
        P(),
        P(None, "mp", None),
        P("mp", None),
        P(DP, None, "mp"),
        P(),
        P(None, "mp"),
        P("mp", None),
        P("mp", None),
        P(DP, None),
        P(DP),
    )
    return jax.shard_map(
        on_device,
        mesh=grid,
        in_specs=placed,
        out_specs=(P(DP, "mp"), P(DP, "mp"), P(DP)),
        check_vma=False,
    )
```

profile of v0, /device:TPU:32, one launch (start us, length us, event | category | flops | bytes accessed | tf_op | source)
XLA Modules:
  0.0 286.8 jit_solution(16037919978966261291)
XLA Ops:
  9.5 11.4 %all_to_all.29 = bf16[8,7,8,128]{3,2,1,0:T(8,128)(2,1)S(1)} all-to-all(bf16[8,7,8,128]{3,2,1,0:T(8,128)(2,1)S(1)} %broadcast_in_dim.16), channel_id=1, replica_groups=mesh['z'=8,'x'=4,'c'=2,'mp'=8] {'mp'}, dimensions={0} | all-to-all | bytes 229376 | tf_op jit(solution)/shard_map/all_to_all | solution.py:93
  21.7 1.3 gather_fusion
  26.5 3.1 %collective-permute-start = (bf16[128,1920]{1,0:T(8,128)(2,1)}, bf16[128,1920]{1,0:T(8,128)(2,1)S(1)}, u32[]{:S(2)}, u32[]{:S(2)}) collective-permute-start(bf16[128,1920]{1,0:T(8,128)(2,1)} %get-tuple-element.14), channel_id=1, source_target_pairs={{0,1},{1,2},{2,3},{3,4},{4,5},{5,6},{6,7},{7,0},{8,9},{9,10},{10,1... | collective-permute-start | bytes 1474568 | tf_op jit(solution)/shard_map/ppermute | solution.py:39
  29.6 4.0 %collective-permute-start.4 = (bf16[128,1920]{1,0:T(8,128)(2,1)}, bf16[128,1920]{1,0:T(8,128)(2,1)S(1)}, u32[]{:S(2)}, u32[]{:S(2)}) collective-permute-start(bf16[128,1920]{1,0:T(8,128)(2,1)} %get-tuple-element.14), channel_id=1, source_target_pairs={{0,7},{1,0},{2,1},{3,2},{4,3},{5,4},{6,5},{7,6},{8,15},{9,8},{10,9... | collective-permute-start | bytes 1474568 | tf_op jit(solution)/shard_map/ppermute | solution.py:42
  33.7 3.0 %pad.10 = bf16[3,2,128,1408]{3,2,1,0:T(8,128)(2,1)} pad(bf16[3,2,88,1408]{3,2,1,0:T(8,128)(2,1)} %bitcast.200, bf16[]{:T(256)} %constant.228.clone.1), padding=0_0x0_0x0_40x0_0 | pad | bytes 3649538 | tf_op jit(solution)/shard_map/jit(_pad)/pad | solution.py:110
  38.7 3.1 %fusion.18 = bf16[1024,768]{1,0:T(8,128)(2,1)} fusion(bf16[768,1408]{1,0:T(8,128)(2,1)} %bitcast.192, bf16[1,128,1408]{2,1,0:T(8,128)(2,1)S(1)} %copy-done.5, f32[1408]{0:T(1024)S(1)} %copy-done.16, f32[128]{0:T(128)S(1)} %add_rsqrt_fusion.9, f32[128]{0:T(128)S(1)} %broadcast_multiply_fusion.8), kind=kOutput, calls=%fused_computation.44 | convolution fusion | flops 277823488 | bytes 2726400 | tf_op jit(solution)/shard_map/pi,oi->po/dot_general | solution.py:117
  43.0 2.8 collective-permute-start.1
  45.7 4.3 %collective-permute-start.5 = (bf16[128,1920]{1,0:T(8,128)(2,1)S(1)}, bf16[128,1920]{1,0:T(8,128)(2,1)S(1)}, u32[]{:S(2)}, u32[]{:S(2)}) collective-permute-start(bf16[128,1920]{1,0:T(8,128)(2,1)S(1)} %collective-permute-done.4), channel_id=1, source_target_pairs={{0,7},{1,0},{2,1},{3,2},{4,3},{5,4},{6,5},{7,6},{8,15},{9,8},{10,9... | collective-permute-start | bytes 1474568 | tf_op jit(solution)/shard_map/ppermute | solution.py:42
  50.9 3.2 %fusion.17 = bf16[1024,768]{1,0:T(8,128)(2,1)} fusion(bf16[1024,768]{1,0:T(8,128)(2,1)} %fusion.18, bf16[768,1408]{1,0:T(8,128)(2,1)} %bitcast.193, f32[1408]{0:T(1024)S(1)} %copy-done.16, f32[128]{0:T(128)S(1)} %add_rsqrt_fusion.8, f32[128]{0:T(128)S(1)} %broadcast_multiply_fusion.7, bf16[128,1920]{1,0:T(8,128)(2,1)S(1)} %collective-permute-done), kind=kOutput, calls=%fused_computation.42 | convolution fusion | flops 277823488 | bytes 2728960 | tf_op jit(solution)/shard_map/pi,oi->po/dot_general | solution.py:117
  56.6 1.4 collective-permute-done.5
  58.1 4.6 %collective-permute-start.2 = (bf16[128,1920]{1,0:T(8,128)(2,1)S(1)}, bf16[128,1920]{1,0:T(8,128)(2,1)S(1)}, u32[]{:S(2)}, u32[]{:S(2)}) collective-permute-start(bf16[128,1920]{1,0:T(8,128)(2,1)S(1)} %collective-permute-done.1), channel_id=1, source_target_pairs={{0,1},{1,2},{2,3},{3,4},{4,5},{5,6},{6,7},{7,0},{8,9},{9,10},{10,1... | collective-permute-start | bytes 1474568 | tf_op jit(solution)/shard_map/ppermute | solution.py:39
  62.7 2.5 collective-permute-start.6
  67.6 2.6 collective-permute-done.2
  70.7 2.7 collective-permute-done.6
  73.5 4.5 %collective-permute-start.3 = (bf16[128,1920]{1,0:T(8,128)(2,1)S(1)}, bf16[128,1920]{1,0:T(8,128)(2,1)S(1)}, u32[]{:S(2)}, u32[]{:S(2)}) collective-permute-start(bf16[128,1920]{1,0:T(8,128)(2,1)S(1)} %collective-permute-done.2), channel_id=1, source_target_pairs={{0,1},{1,2},{2,3},{3,4},{4,5},{5,6},{6,7},{7,0},{8,9},{9,10},{10,1... | collective-permute-start | bytes 1474568 | tf_op jit(solution)/shard_map/ppermute | solution.py:39
  80.5 5.0 %collective-permute-done.3 = bf16[128,1920]{1,0:T(8,128)(2,1)S(1)} collective-permute-done((bf16[128,1920]{1,0:T(8,128)(2,1)S(1)}, bf16[128,1920]{1,0:T(8,128)(2,1)S(1)}, u32[]{:S(2)}, u32[]{:S(2)}) %collective-permute-start.3) | collective-permute-done | bytes 491552 | tf_op jit(solution)/shard_map/ppermute | solution.py:39
  90.2 2.1 copy.52
  92.2 1.9 gather_fusion.2
  94.2 1.8 fusion.70
  97.9 5.7 %fusion.19 = bf16[512,2,128]{0,2,1:T(8,128)(2,1)S(1)} fusion(bf16[1024,2,128]{0,2,1:T(8,128)(2,1)S(1)} %bitcast.205, f32[2,512]{1,0:T(2,128)S(1)} %fusion.164, f32[2,512,1024]{2,1,0:T(8,128)} %copy-done.2), kind=kOutput, calls=%fused_computation.45 | convolution fusion | flops 273811456 | bytes 4984832 | tf_op jit(solution)/shard_map/hsp,phd->shd/dot_general | solution.py:126
  104.6 7.4 %all-to-all-start.2 = ((bf16[8,64,176]{2,1,0:T(8,128)(2,1)}), bf16[8,64,176]{2,1,0:T(8,128)(2,1)S(1)}, u32[]{:S(2)}, u32[]{:S(2)}) async-start(bf16[8,64,176]{2,1,0:T(8,128)(2,1)} %reshape.519), calls=%async_computation.2 | async-start | bytes 524288 | tf_op jit(solution)/shard_map/all_to_all | solution.py:128
  112.1 1.6 fusion.131
  115.6 1.6 dynamic-slice_dynamic-update-slice_fusion.15
  117.2 1.6 dynamic-slice_dynamic-update-slice_fusion.14
  118.7 1.6 dynamic-slice_dynamic-update-slice_fusion.13
  120.3 1.6 dynamic-slice_dynamic-update-slice_fusion.12
  121.9 1.6 dynamic-slice_dynamic-update-slice_fusion.11
  123.4 1.6 dynamic-slice_dynamic-update-slice_fusion.10
  125.0 1.6 dynamic-slice_dynamic-update-slice_fusion.9
  126.6 1.6 dynamic-slice_dynamic-update-slice_fusion.8
  128.1 1.3 reshape.503
  131.4 7.4 %fusion.5 = f32[4,128]{1,0:T(4,128)S(1)} fusion(f32[4,128]{1,0:T(4,128)S(1)} %get-tuple-element.24, bf16[8,128,4,128]{3,2,1,0:T(4,128)(2,1)S(1)} %reshape.503), kind=kLoop, calls=%fused_computation.15 | loop fusion | flops 2096640 | bytes 1052672 | tf_op jit(solution)/shard_map/reduce_sum | solution.py:17
  138.9 1.8 multiply_convert_fusion.1
  140.6 1.3 copy.76
  141.9 1.7 convolution_convert_fusion.2
  143.6 7.3 %all-to-all-start = ((bf16[8,64,1024]{2,1,0:T(8,128)(2,1)}), bf16[8,64,1024]{2,1,0:T(8,128)(2,1)S(1)}, u32[]{:S(2)}, u32[]{:S(2)}) async-start(bf16[8,64,1024]{2,1,0:T(8,128)(2,1)} %bitcast.202), calls=%async_computation | async-start | bytes 2097152 | tf_op jit(solution)/shard_map/all_to_all | solution.py:106
  151.0 1.8 slice_dynamic-update-slice_fusion.3
  152.7 1.8 slice_dynamic-update-slice_fusion.2
  156.0 3.1 %gather_fusion.1 = bf16[64,1408]{1,0:T(8,128)(2,1)S(1)} fusion(bf16[1024,1408]{1,0:T(8,128)(2,1)} %slice_dynamic-update-slice_fusion, s32[1024]{0:T(1024)S(1)} %pad_clamp_fusion.1), kind=kCustom, calls=%fused_computation.1 | custom fusion | bytes 360704 | tf_op jit(solution)/shard_map/gather | solution.py:133
  159.5 8.6 %all-to-all-done = bf16[8,64,1024]{2,1,0:T(8,128)(2,1)S(1)} async-done(((bf16[8,64,1024]{2,1,0:T(8,128)(2,1)}), bf16[8,64,1024]{2,1,0:T(8,128)(2,1)S(1)}, u32[]{:S(2)}, u32[]{:S(2)}) %all-to-all-start) | async-done | bytes 1048608 | tf_op jit(solution)/shard_map/all_to_all | solution.py:106
  168.3 2.0 slice.146
  170.4 1.6 copy-done.1
  171.9 1.9 fusion.127
  173.8 17.0 %all-gather.5.cloned.1.call-done = bf16[8,256,8,128]{3,2,1,0:T(8,128)(2,1)} async-done(((bf16[8,4,8,128]{3,2,1,0:T(8,128)(2,1)}), bf16[8,256,8,128]{3,2,1,0:T(8,128)(2,1)}) %all-gather.5.cloned.1.call-update) | async-done | bytes 4194320 | tf_op jit(solution)/shard_map/all_gather | solution.py:94
  190.8 2.1 slice-done
  192.9 1.3 fusion.165
  194.6 2.5 convolution_convert_fusion.11
  197.1 2.5 collective-permute-start.7
  199.6 4.5 %collective-permute-start.11 = (bf16[64,1152]{1,0:T(8,128)(2,1)S(1)}, bf16[64,1152]{1,0:T(8,128)(2,1)S(1)}, u32[]{:S(2)}, u32[]{:S(2)}) collective-permute-start(bf16[64,1152]{1,0:T(8,128)(2,1)S(1)} %fusion.126), channel_id=1, source_target_pairs={{0,7},{1,0},{2,1},{3,2},{4,3},{5,4},{6,5},{7,6},{8,15},{9,8},{10,9... | collective-permute-start | bytes 442376 | tf_op jit(solution)/shard_map/ppermute | solution.py:42
  204.2 2.0 collective-permute-done.7
  206.2 1.9 collective-permute-start.8
  208.2 5.3 %collective-permute-start.12 = (bf16[64,1152]{1,0:T(8,128)(2,1)S(1)}, bf16[64,1152]{1,0:T(8,128)(2,1)S(1)}, u32[]{:S(2)}, u32[]{:S(2)}) collective-permute-start(bf16[64,1152]{1,0:T(8,128)(2,1)S(1)} %collective-permute-done.11), channel_id=1, source_target_pairs={{0,7},{1,0},{2,1},{3,2},{4,3},{5,4},{6,5},{7,6},{8,15},{9,8},{10,9... | collective-permute-start | bytes 442376 | tf_op jit(solution)/shard_map/ppermute | solution.py:42
  214.5 1.9 collective-permute-start.9
  216.5 5.2 %collective-permute-start.13 = (bf16[64,1152]{1,0:T(8,128)(2,1)S(1)}, bf16[64,1152]{1,0:T(8,128)(2,1)S(1)}, u32[]{:S(2)}, u32[]{:S(2)}) collective-permute-start(bf16[64,1152]{1,0:T(8,128)(2,1)S(1)} %collective-permute-done.12), channel_id=1, source_target_pairs={{0,7},{1,0},{2,1},{3,2},{4,3},{5,4},{6,5},{7,6},{8,15},{9,8},{10,9... | collective-permute-start | bytes 442376 | tf_op jit(solution)/shard_map/ppermute | solution.py:42
  222.8 2.2 collective-permute-start.10
  225.0 6.0 %collective-permute-done.10 = bf16[64,1152]{1,0:T(8,128)(2,1)S(1)} collective-permute-done((bf16[64,1152]{1,0:T(8,128)(2,1)S(1)}, bf16[64,1152]{1,0:T(8,128)(2,1)S(1)}, u32[]{:S(2)}, u32[]{:S(2)}) %collective-permute-start.10) | collective-permute-done | bytes 147488 | tf_op jit(solution)/shard_map/ppermute | solution.py:39
  232.4 3.3 %convolution_convert_fusion.1 = bf16[1024,512]{1,0:T(8,128)(2,1)S(1)} fusion(bf16[512,1024]{1,0:T(8,128)(2,1)S(1)} %copy-done, f32[512,512]{1,0:T(8,128)} %get-tuple-element.28, bf16[512,1152]{1,0:T(8,128)(2,1)} %bitcast.210, f32[1024]{0:T(1024)S(1)} %copy-done.17, f32[512]{0:T(512)S(1)} %rsqrt_bitcast_fusion, f32[512]{0:T(512)S(1)} %get-tuple-element.23, ...), kind=kOutput, calls=%fused_computation.24 | convolution fusion | flops 1079508992 | bytes 5251072 | tf_op jit(solution)/shard_map/rd,rh->dh/dot_general | solution.py:155
  236.9 1.9 collective-permute-start.14
  238.8 3.0 %collective-permute-done.14 = bf16[32,32,512]{2,1,0:T(8,128)(2,1)} collective-permute-done((bf16[32,32,512]{2,1,0:T(8,128)(2,1)}, bf16[32,32,512]{2,1,0:T(8,128)(2,1)}, u32[]{:S(2)}, u32[]{:S(2)}) %collective-permute-start.14) | collective-permute-done | bytes 1048608 | tf_op jit(solution)/shard_map/ppermute | solution.py:161
  241.7 1.6 fusion.6
  243.4 19.2 %all_to_all.30 = bf16[1,8,4,32,512]{4,3,1,0,2:T(8,128)(2,1)S(1)} all-to-all(bf16[1,8,4,32,512]{4,3,1,0,2:T(8,128)(2,1)S(1)} %copy.51), channel_id=1, replica_groups=mesh['z'=8,'x'=4,'c'=2,'mp'=8] {'x'}, dimensions={2} | all-to-all | bytes 2097152 | tf_op jit(solution)/shard_map/all_to_all | solution.py:164
  263.6 5.0 %all-to-all-start.4 = ((bf16[8,32,512]{2,1,0:T(8,128)(2,1)}), bf16[8,32,512]{2,1,0:T(8,128)(2,1)S(1)}, u32[]{:S(2)}, u32[]{:S(2)}) async-start(bf16[8,32,512]{2,1,0:T(8,128)(2,1)} %reduce_sum.260), calls=%async_computation.4 | async-start | bytes 524288 | tf_op jit(solution)/shard_map/all_to_all | solution.py:166
  268.6 1.6 convert_reduce_fusion.11
  270.1 9.2 %all-to-all-done.4 = bf16[8,32,512]{2,1,0:T(8,128)(2,1)S(1)} async-done(((bf16[8,32,512]{2,1,0:T(8,128)(2,1)}), bf16[8,32,512]{2,1,0:T(8,128)(2,1)S(1)}, u32[]{:S(2)}, u32[]{:S(2)}) %all-to-all-start.4) | async-done | bytes 262176 | tf_op jit(solution)/shard_map/all_to_all | solution.py:166
  (163 shorter events, 38.1 us)
Async XLA Ops:
  7.2 134.8 %copy-start = (bf16[512,1024]{1,0:T(8,128)(2,1)S(1)}, bf16[512,1024]{1,0:T(8,128)(2,1)}, u32[]{:S(2)}) copy-start(bf16[512,1024]{1,0:T(8,128)(2,1)} %param.18) | copy-start | bytes 3145732
  7.2 14.4 %copy-start.14 = (s32[1,512]{1,0:T(1,128)S(1)}, s32[1,512]{1,0:T(1,128)}, u32[]{:S(2)}) copy-start(s32[1,512]{1,0:T(1,128)} %param.20) | copy-start | bytes 6148
  7.2 14.5 %copy-start.3 = (bf16[1,1024,128]{2,1,0:T(8,128)(2,1)S(1)}, bf16[1,1024,128]{2,1,0:T(8,128)(2,1)}, u32[]{:S(2)}) copy-start(bf16[1,1024,128]{2,1,0:T(8,128)(2,1)} %param.15) | copy-start | bytes 786436
  7.2 15.8 %copy-start.5 = (bf16[1,128,1408]{2,1,0:T(8,128)(2,1)S(1)}, bf16[1,128,1408]{2,1,0:T(8,128)(2,1)}, u32[]{:S(2)}) copy-start(bf16[1,128,1408]{2,1,0:T(8,128)(2,1)} %param.11) | copy-start | bytes 1081348
  7.2 161.1 %all-gather.3.cloned.1.call-start = ((), (), s32[]{:S(2)}) async-start(), calls=%async_computation.5 | async-start | bytes 3194880 | tf_op jit(solution)/shard_map/all_gather | solution.py:95
  21.6 169.2 %all-gather.5.cloned.1.call-start = ((), (), s32[]{:S(2)}) async-start(), calls=%async_computation.6 | async-start | bytes 4259840 | tf_op jit(solution)/shard_map/all_gather | solution.py:94
  26.5 15.9 %collective-permute-start = (bf16[128,1920]{1,0:T(8,128)(2,1)}, bf16[128,1920]{1,0:T(8,128)(2,1)S(1)}, u32[]{:S(2)}, u32[]{:S(2)}) collective-permute-start(bf16[128,1920]{1,0:T(8,128)(2,1)} %get-tuple-element.14), channel_id=1, source_target_pairs={{0,1},{1,2},{2,3},{3,4},{4,5},{5,6},{6,7},{7,0},{8,9},{9,10},{10,1... | collective-permute-start | bytes 1474568 | tf_op jit(solution)/shard_map/ppermute | solution.py:39
  29.6 13.3 %collective-permute-start.4 = (bf16[128,1920]{1,0:T(8,128)(2,1)}, bf16[128,1920]{1,0:T(8,128)(2,1)S(1)}, u32[]{:S(2)}, u32[]{:S(2)}) collective-permute-start(bf16[128,1920]{1,0:T(8,128)(2,1)} %get-tuple-element.14), channel_id=1, source_target_pairs={{0,7},{1,0},{2,1},{3,2},{4,3},{5,4},{6,5},{7,6},{8,15},{9,8},{10,9... | collective-permute-start | bytes 1474568 | tf_op jit(solution)/shard_map/ppermute | solution.py:42
  33.7 5.0 %copy-start.16 = (f32[1408]{0:T(1024)S(1)}, f32[1408]{0:T(1024)}, u32[]{:S(2)}) copy-start(f32[1408]{0:T(1024)} %param.12) | copy-start | bytes 16900
  43.0 13.2 %collective-permute-start.1 = (bf16[128,1920]{1,0:T(8,128)(2,1)S(1)}, bf16[128,1920]{1,0:T(8,128)(2,1)S(1)}, u32[]{:S(2)}, u32[]{:S(2)}) collective-permute-start(bf16[128,1920]{1,0:T(8,128)(2,1)S(1)} %collective-permute-done), channel_id=1, source_target_pairs={{0,1},{1,2},{2,3},{3,4},{4,5},{5,6},{6,7},{7,0},{8,9},{9,10},{10,1... | collective-permute-start | bytes 1474568 | tf_op jit(solution)/shard_map/ppermute | solution.py:39
  45.7 12.2 %collective-permute-start.5 = (bf16[128,1920]{1,0:T(8,128)(2,1)S(1)}, bf16[128,1920]{1,0:T(8,128)(2,1)S(1)}, u32[]{:S(2)}, u32[]{:S(2)}) collective-permute-start(bf16[128,1920]{1,0:T(8,128)(2,1)S(1)} %collective-permute-done.4), channel_id=1, source_target_pairs={{0,7},{1,0},{2,1},{3,2},{4,3},{5,4},{6,5},{7,6},{8,15},{9,8},{10,9... | collective-permute-start | bytes 1474568 | tf_op jit(solution)/shard_map/ppermute | solution.py:42
  50.9 15.1 %copy-start.10 = (bf16[3,2,128,1408]{3,2,1,0:T(8,128)(2,1)S(1)}, bf16[3,2,128,1408]{3,2,1,0:T(8,128)(2,1)}, u32[]{:S(2)}) copy-start(bf16[3,2,128,1408]{3,2,1,0:T(8,128)(2,1)} %pad.10) | copy-start | bytes 6488068
  54.2 11.9 %copy-start.11 = (bf16[1024,768]{1,0:T(8,128)(2,1)S(1)}, bf16[1024,768]{1,0:T(8,128)(2,1)}, u32[]{:S(2)}) copy-start(bf16[1024,768]{1,0:T(8,128)(2,1)} %fusion.17) | copy-start | bytes 4718596
  58.0 56.3 %copy-start.6 = (bf16[128,1920]{1,0:T(8,128)(2,1)}, bf16[128,1920]{1,0:T(8,128)(2,1)S(1)}, u32[]{:S(2)}) copy-start(bf16[128,1920]{1,0:T(8,128)(2,1)S(1)} %collective-permute-done.5) | copy-start | bytes 1474564
  58.1 12.2 %collective-permute-start.2 = (bf16[128,1920]{1,0:T(8,128)(2,1)S(1)}, bf16[128,1920]{1,0:T(8,128)(2,1)S(1)}, u32[]{:S(2)}, u32[]{:S(2)}) collective-permute-start(bf16[128,1920]{1,0:T(8,128)(2,1)S(1)} %collective-permute-done.1), channel_id=1, source_target_pairs={{0,1},{1,2},{2,3},{3,4},{4,5},{5,6},{6,7},{7,0},{8,9},{9,10},{10,1... | collective-permute-start | bytes 1474568 | tf_op jit(solution)/shard_map/ppermute | solution.py:39
  62.7 10.7 %collective-permute-start.6 = (bf16[128,1920]{1,0:T(8,128)(2,1)S(1)}, bf16[128,1920]{1,0:T(8,128)(2,1)S(1)}, u32[]{:S(2)}, u32[]{:S(2)}) collective-permute-start(bf16[128,1920]{1,0:T(8,128)(2,1)S(1)} %collective-permute-done.5), channel_id=1, source_target_pairs={{0,7},{1,0},{2,1},{3,2},{4,3},{5,4},{6,5},{7,6},{8,15},{9,8},{10,9... | collective-permute-start | bytes 1474568 | tf_op jit(solution)/shard_map/ppermute | solution.py:42
  73.4 40.2 %copy-start.8 = (bf16[128,1920]{1,0:T(8,128)(2,1)}, bf16[128,1920]{1,0:T(8,128)(2,1)S(1)}, u32[]{:S(2)}) copy-start(bf16[128,1920]{1,0:T(8,128)(2,1)S(1)} %collective-permute-done.6) | copy-start | bytes 1474564
  73.5 11.9 %collective-permute-start.3 = (bf16[128,1920]{1,0:T(8,128)(2,1)S(1)}, bf16[128,1920]{1,0:T(8,128)(2,1)S(1)}, u32[]{:S(2)}, u32[]{:S(2)}) collective-permute-start(bf16[128,1920]{1,0:T(8,128)(2,1)S(1)} %collective-permute-done.2), channel_id=1, source_target_pairs={{0,1},{1,2},{2,3},{3,4},{4,5},{5,6},{6,7},{7,0},{8,9},{9,10},{10,1... | collective-permute-start | bytes 1474568 | tf_op jit(solution)/shard_map/ppermute | solution.py:39
  85.5 2.0 copy-start.9
  96.0 1.9 copy-start.2
  96.0 1.9 copy-start.12
  104.6 39.0 %all-to-all-start.2 = ((bf16[8,64,176]{2,1,0:T(8,128)(2,1)}), bf16[8,64,176]{2,1,0:T(8,128)(2,1)S(1)}, u32[]{:S(2)}, u32[]{:S(2)}) async-start(bf16[8,64,176]{2,1,0:T(8,128)(2,1)} %reshape.519), calls=%async_computation.2 | async-start | bytes 524288 | tf_op jit(solution)/shard_map/all_to_all | solution.py:128
  129.5 9.4 %copy-start.15 = (bf16[1024,512]{1,0:T(8,128)(2,1)S(1)}, bf16[1024,512]{1,0:T(8,128)(2,1)}, u32[]{:S(2)}) copy-start(bf16[1024,512]{1,0:T(8,128)(2,1)} %param.17) | copy-start | bytes 3145732
  129.5 9.4 %copy-start.17 = (f32[1024]{0:T(1024)S(1)}, f32[1024]{0:T(1024)}, u32[]{:S(2)}) copy-start(f32[1024]{0:T(1024)} %param.16) | copy-start | bytes 12292
  130.2 10.5 %copy-start.4 = (bf16[8,128,4,128]{3,0,1,2:T(8,128)(2,1)}, bf16[8,128,4,128]{3,0,1,2:T(8,128)(2,1)S(1)}, u32[]{:S(2)}) copy-start(bf16[8,128,4,128]{3,0,1,2:T(8,128)(2,1)S(1)} %copy.42) | copy-start | bytes 3145732
  140.6 1.3 copy-start.18
  143.6 10.9 %copy-start.7 = (bf16[128,1920]{1,0:T(8,128)(2,1)S(1)}, bf16[128,1920]{1,0:T(8,128)(2,1)}, u32[]{:S(2)}) copy-start(bf16[128,1920]{1,0:T(8,128)(2,1)} %copy-done.6) | copy-start | bytes 1474564
  143.6 24.5 %all-to-all-start = ((bf16[8,64,1024]{2,1,0:T(8,128)(2,1)}), bf16[8,64,1024]{2,1,0:T(8,128)(2,1)S(1)}, u32[]{:S(2)}, u32[]{:S(2)}) async-start(bf16[8,64,1024]{2,1,0:T(8,128)(2,1)} %bitcast.202), calls=%async_computation | async-start | bytes 2097152 | tf_op jit(solution)/shard_map/all_to_all | solution.py:106
  170.4 1.6 copy-start.1
  190.8 2.1 slice-start
  197.1 9.1 %collective-permute-start.7 = (bf16[64,1152]{1,0:T(8,128)(2,1)S(1)}, bf16[64,1152]{1,0:T(8,128)(2,1)S(1)}, u32[]{:S(2)}, u32[]{:S(2)}) collective-permute-start(bf16[64,1152]{1,0:T(8,128)(2,1)S(1)} %fusion.126), channel_id=1, source_target_pairs={{0,1},{1,2},{2,3},{3,4},{4,5},{5,6},{6,7},{7,0},{8,9},{9,10},{10,1... | collective-permute-start | bytes 442376 | tf_op jit(solution)/shard_map/ppermute | solution.py:39
  199.6 8.6 %collective-permute-start.11 = (bf16[64,1152]{1,0:T(8,128)(2,1)S(1)}, bf16[64,1152]{1,0:T(8,128)(2,1)S(1)}, u32[]{:S(2)}, u32[]{:S(2)}) collective-permute-start(bf16[64,1152]{1,0:T(8,128)(2,1)S(1)} %fusion.126), channel_id=1, source_target_pairs={{0,7},{1,0},{2,1},{3,2},{4,3},{5,4},{6,5},{7,6},{8,15},{9,8},{10,9... | collective-permute-start | bytes 442376 | tf_op jit(solution)/shard_map/ppermute | solution.py:42
  206.2 8.3 %collective-permute-start.8 = (bf16[64,1152]{1,0:T(8,128)(2,1)S(1)}, bf16[64,1152]{1,0:T(8,128)(2,1)S(1)}, u32[]{:S(2)}, u32[]{:S(2)}) collective-permute-start(bf16[64,1152]{1,0:T(8,128)(2,1)S(1)} %collective-permute-done.7), channel_id=1, source_target_pairs={{0,1},{1,2},{2,3},{3,4},{4,5},{5,6},{6,7},{7,0},{8,9},{9,10},{10,1... | collective-permute-start | bytes 442376 | tf_op jit(solution)/shard_map/ppermute | solution.py:39
  208.2 23.2 %copy-start.19 = (bf16[512,512]{1,0:T(8,128)(2,1)S(1)}, bf16[512,512]{1,0:T(8,128)(2,1)}, u32[]{:S(2)}) copy-start(bf16[512,512]{1,0:T(8,128)(2,1)} %copy-done.18) | copy-start | bytes 1572868
  208.2 8.3 %collective-permute-start.12 = (bf16[64,1152]{1,0:T(8,128)(2,1)S(1)}, bf16[64,1152]{1,0:T(8,128)(2,1)S(1)}, u32[]{:S(2)}, u32[]{:S(2)}) collective-permute-start(bf16[64,1152]{1,0:T(8,128)(2,1)S(1)} %collective-permute-done.11), channel_id=1, source_target_pairs={{0,7},{1,0},{2,1},{3,2},{4,3},{5,4},{6,5},{7,6},{8,15},{9,8},{10,9... | collective-permute-start | bytes 442376 | tf_op jit(solution)/shard_map/ppermute | solution.py:42
  214.5 8.2 %collective-permute-start.9 = (bf16[64,1152]{1,0:T(8,128)(2,1)S(1)}, bf16[64,1152]{1,0:T(8,128)(2,1)S(1)}, u32[]{:S(2)}, u32[]{:S(2)}) collective-permute-start(bf16[64,1152]{1,0:T(8,128)(2,1)S(1)} %collective-permute-done.8), channel_id=1, source_target_pairs={{0,1},{1,2},{2,3},{3,4},{4,5},{5,6},{6,7},{7,0},{8,9},{9,10},{10,1... | collective-permute-start | bytes 442376 | tf_op jit(solution)/shard_map/ppermute | solution.py:39
  216.5 14.5 %collective-permute-start.13 = (bf16[64,1152]{1,0:T(8,128)(2,1)S(1)}, bf16[64,1152]{1,0:T(8,128)(2,1)S(1)}, u32[]{:S(2)}, u32[]{:S(2)}) collective-permute-start(bf16[64,1152]{1,0:T(8,128)(2,1)S(1)} %collective-permute-done.12), channel_id=1, source_target_pairs={{0,7},{1,0},{2,1},{3,2},{4,3},{5,4},{6,5},{7,6},{8,15},{9,8},{10,9... | collective-permute-start | bytes 442376 | tf_op jit(solution)/shard_map/ppermute | solution.py:42
  222.8 8.2 %collective-permute-start.10 = (bf16[64,1152]{1,0:T(8,128)(2,1)S(1)}, bf16[64,1152]{1,0:T(8,128)(2,1)S(1)}, u32[]{:S(2)}, u32[]{:S(2)}) collective-permute-start(bf16[64,1152]{1,0:T(8,128)(2,1)S(1)} %collective-permute-done.9), channel_id=1, source_target_pairs={{0,1},{1,2},{2,3},{3,4},{4,5},{5,6},{6,7},{7,0},{8,9},{9,10},{10,1... | collective-permute-start | bytes 442376 | tf_op jit(solution)/shard_map/ppermute | solution.py:39
  231.3 1.1 copy-start.13
  236.9 4.9 %collective-permute-start.14 = (bf16[32,32,512]{2,1,0:T(8,128)(2,1)}, bf16[32,32,512]{2,1,0:T(8,128)(2,1)}, u32[]{:S(2)}, u32[]{:S(2)}) collective-permute-start(bf16[32,32,512]{2,1,0:T(8,128)(2,1)} %fusion.25), channel_id=1, source_target_pairs={{0,8},{8,0},{1,9},{9,1},{2,10},{10,2},{3,11},{11,3},{4,12},{12,4},... | collective-permute-start | bytes 3145736 | tf_op jit(solution)/shard_map/ppermute | solution.py:161
  263.6 15.7 %all-to-all-start.4 = ((bf16[8,32,512]{2,1,0:T(8,128)(2,1)}), bf16[8,32,512]{2,1,0:T(8,128)(2,1)S(1)}, u32[]{:S(2)}, u32[]{:S(2)}) async-start(bf16[8,32,512]{2,1,0:T(8,128)(2,1)} %reduce_sum.260), calls=%async_computation.4 | async-start | bytes 524288 | tf_op jit(solution)/shard_map/all_to_all | solution.py:166
Sparse Core Ops, SparseCore 0:
  21.7 84.0 all-gather.2
  109.0 81.6 all-gather.4
where the time goes:
time: 288 us; the launch traced here: 287 us
  starting transfers between devices  70.9 us (25%)
  waiting for transfers between devices  60.9 us (21%)
  local copies, waits for them, and re-layouts  57.7 us (20%)
  matrix products  31.6 us (11%)
  blocking collectives  30.6 us (11%)
  other arithmetic  19.4 us (7%)
  between operations  15.7 us (5%)
    unnamed x77, local copies, waits for them, and re-layouts  29.5 us
    ppermute x6, starting transfers between devices, ring(): left = lax.ppermute(left, 'mp', shift(-1))  25.8 us
    ppermute x8, starting transfers between devices, ring(): right = lax.ppermute(right, 'mp', shift(1))  23.4 us
    all_to_all x1, blocking collectives, on_device(): kept = lax.all_to_all(kept, 'x', 1, 0, tiled=False)  19.2 us
    ppermute x8, waiting for transfers between devices, ring(): right = lax.ppermute(right, 'mp', shift(1))  19.1 us
    all_gather x1, waiting for transfers between devices, on_device(): lax.all_gather(shares[:, :4], DP, axis=1, tiled=True)  17 us
    all_to_all x1, blocking collectives, on_device(): lax.all_to_all(jnp.broadcast_to(mine, (8, *mine.shape)), 'mp', 0, 0, tile...  11.4 us
    dot_general x8, matrix products, on_device(): jnp.einsum('pi,oi->po', normed, weights, preferred_element_type=F32)  11 us
  transfers between devices with their start and end apart: 20, of which 13 were waited for; matrix products, arithmetic and copies ran while one was open for 31% of the time, Pallas kernels for 0%

commit v1 on v0

--- a/solution.py
+++ b/solution.py
@@ -90,7 +90,20 @@
             lax.dynamic_index_in_dim(to_tiles(target_head, 3), at, 0, False),
         ]
     )
-    shares = lax.all_to_all(jnp.broadcast_to(mine, (8, *mine.shape)), "mp", 0, 0, tiled=True)
+    value_2 = jnp.broadcast_to(mine, (8, *mine.shape))
+    ways, here = (lax.axis_size("mp"), lax.axis_index("mp"))
+    width = value_2.shape[0] // ways
+    shape = list(value_2.shape)
+    shape[0] = width
+    height = shape[0]
+    shape[0] = height * ways
+    full = jnp.zeros(shape, value_2.dtype)
+    for mask in range(ways):
+        part = lax.dynamic_slice_in_dim(value_2, (here ^ mask) * width, width, axis=0)
+        if mask:
+            part = lax.ppermute(part, "mp", [(d, d ^ mask) for d in range(ways)])
+        full = lax.dynamic_update_slice_in_dim(full, part, (here ^ mask) * height, axis=0)
+    shares = full
     out_full = from_tiles(lax.all_gather(shares[:, :4], DP, axis=1, tiled=True), 176, 1408)
     head_full = from_tiles(lax.all_gather(shares[:, 4:], DP, axis=1, tiled=True), 176, 1024)
     rows = student_in[0][picked]

time: 288 us -> 308 us (1.069)
  starting transfers between devices: 70.9 us -> 96.6 us
  blocking collectives: 30.6 us -> 19.4 us
  waiting for transfers between devices: 60.9 us -> 65.2 us
    ppermute x0 -> x7, starting transfers between devices: none -> 26.9 us  [on_device(): part = lax.ppermute(part, 'mp', [(d, d ^ mask) for d in range(ways)])]
    all_to_all x1 -> x0, blocking collectives: 11.4 us -> none  [on_device(): lax.all_to_all(jnp.broadcast_to(mine, (8, *mine.shape)), 'mp', 0, 0, tile...]
    all_gather x1, waiting for transfers between devices: 17 us -> 21.5 us  [on_device(): lax.all_gather(shares[:, :4], DP, axis=1, tiled=True)]
    ppermute x0 -> x7, waiting for transfers between devices: none -> 3.8 us  [on_device(): part = lax.ppermute(part, 'mp', [(d, d ^ mask) for d in range(ways)])]
  transfers between devices with their start and end apart: 20 -> 27, of which waited for: 13 -> 14; matrix products, arithmetic and copies ran while one was open for 31% -> 29% of each run, Pallas kernels for 0% -> 0%
where the time goes in v1:
time: 308 us; the launch traced here: 306 us
  starting transfers between devices  96.6 us (31%)
  waiting for transfers between devices  65.2 us (21%)
  local copies, waits for them, and re-layouts  57.8 us (19%)
  matrix products  31.6 us (10%)
  other arithmetic  19.4 us (6%)
  blocking collectives  19.4 us (6%)
  between operations  15.8 us (5%)
    unnamed x77, local copies, waits for them, and re-layouts  29.5 us
    ppermute x7, starting transfers between devices, on_device(): part = lax.ppermute(part, 'mp', [(d, d ^ mask) for d in range(ways)])  26.9 us
    ppermute x6, starting transfers between devices, ring(): left = lax.ppermute(left, 'mp', shift(-1))  25.6 us
    ppermute x8, starting transfers between devices, ring(): right = lax.ppermute(right, 'mp', shift(1))  22.8 us
    all_gather x1, waiting for transfers between devices, on_device(): lax.all_gather(shares[:, :4], DP, axis=1, tiled=True)  21.5 us
    all_to_all x1, blocking collectives, on_device(): kept = lax.all_to_all(kept, 'x', 1, 0, tiled=False)  19.4 us
    ppermute x8, waiting for transfers between devices, ring(): right = lax.ppermute(right, 'mp', shift(1))  18.4 us
    dot_general x8, matrix products, on_device(): jnp.einsum('pi,oi->po', normed, weights, preferred_element_type=F32)  11 us
  transfers between devices with their start and end apart: 27, of which 14 were waited for; matrix products, arithmetic and copies ran while one was open for 29% of the time, Pallas kernels for 0%

profile of v1, /device:TPU:32, one launch (start us, length us, event | category | flops | bytes accessed | tf_op | source)
XLA Modules:
  0.0 306.0 jit_solution(9101195360426113619)
XLA Ops:
  9.5 2.6 collective-permute-start.7
  12.1 2.7 collective-permute-start.8
  14.8 4.8 %collective-permute-start.9 = (bf16[1,7,8,128]{3,2,1,0:T(8,128)(2,1)S(1)}, bf16[1,7,8,128]{3,2,1,0:T(8,128)(2,1)S(1)}, u32[]{:S(2)}, u32[]{:S(2)}) collective-permute-start(bf16[1,7,8,128]{3,2,1,0:T(8,128)(2,1)S(1)} %maximum_bitcast_fusion.1), channel_id=1, source_target_pairs={{0,3},{1,2},{2,1},{3,0},{4,7},{5,6},{6,5},{7,4},{8,11},{9,10},{10,... | collective-permute-start | bytes 43016 | tf_op jit(solution)/shard_map/ppermute | solution.py:104
  19.6 7.4 %collective-permute-start.10 = (bf16[1,7,8,128]{3,2,1,0:T(8,128)(2,1)S(1)}, bf16[1,7,8,128]{3,2,1,0:T(8,128)(2,1)S(1)}, u32[]{:S(2)}, u32[]{:S(2)}) collective-permute-start(bf16[1,7,8,128]{3,2,1,0:T(8,128)(2,1)S(1)} %maximum_bitcast_fusion.1), channel_id=1, source_target_pairs={{0,4},{1,5},{2,6},{3,7},{4,0},{5,1},{6,2},{7,3},{8,12},{9,13},{10,... | collective-permute-start | bytes 43016 | tf_op jit(solution)/shard_map/ppermute | solution.py:104
  27.0 1.9 collective-permute-start.11
  29.1 4.6 %collective-permute-start.12 = (bf16[1,7,8,128]{3,2,1,0:T(8,128)(2,1)S(1)}, bf16[1,7,8,128]{3,2,1,0:T(8,128)(2,1)S(1)}, u32[]{:S(2)}, u32[]{:S(2)}) collective-permute-start(bf16[1,7,8,128]{3,2,1,0:T(8,128)(2,1)S(1)} %maximum_bitcast_fusion.1), channel_id=1, source_target_pairs={{0,6},{1,7},{2,4},{3,5},{4,2},{5,3},{6,0},{7,1},{8,14},{9,15},{10,... | collective-permute-start | bytes 43016 | tf_op jit(solution)/shard_map/ppermute | solution.py:104
  33.7 2.9 collective-permute-start.13
  36.8 3.7 %collective-permute-done.13 = bf16[1,7,8,128]{3,2,1,0:T(8,128)(2,1)S(1)} collective-permute-done((bf16[1,7,8,128]{3,2,1,0:T(8,128)(2,1)S(1)}, bf16[1,7,8,128]{3,2,1,0:T(8,128)(2,1)S(1)}, u32[]{:S(2)}, u32[]{:S(2)}) %collective-permute-start.13) | collective-permute-done | bytes 14368 | tf_op jit(solution)/shard_map/ppermute | solution.py:104
  46.1 4.3 %collective-permute-start = (bf16[128,1920]{1,0:T(8,128)(2,1)}, bf16[128,1920]{1,0:T(8,128)(2,1)S(1)}, u32[]{:S(2)}, u32[]{:S(2)}) collective-permute-start(bf16[128,1920]{1,0:T(8,128)(2,1)} %get-tuple-element.14), channel_id=1, source_target_pairs={{0,1},{1,2},{2,3},{3,4},{4,5},{5,6},{6,7},{7,0},{8,9},{9,10},{10,1... | collective-permute-start | bytes 1474568 | tf_op jit(solution)/shard_map/ppermute | solution.py:39
  50.4 2.8 collective-permute-start.4
  53.3 3.0 pad.10
  58.3 3.1 %fusion.18 = bf16[1024,768]{1,0:T(8,128)(2,1)} fusion(bf16[768,1408]{1,0:T(8,128)(2,1)} %bitcast.196, bf16[1,128,1408]{2,1,0:T(8,128)(2,1)S(1)} %copy-done.5, f32[1408]{0:T(1024)S(1)} %copy-done.16, f32[128]{0:T(128)S(1)} %add_rsqrt_fusion.9, f32[128]{0:T(128)S(1)} %broadcast_multiply_fusion.8), kind=kOutput, calls=%fused_computation.44 | convolution fusion | flops 277823488 | bytes 2726400 | tf_op jit(solution)/shard_map/pi,oi->po/dot_general | solution.py:130
  62.6 3.1 collective-permute-start.1
  65.6 4.0 %collective-permute-start.5 = (bf16[128,1920]{1,0:T(8,128)(2,1)S(1)}, bf16[128,1920]{1,0:T(8,128)(2,1)S(1)}, u32[]{:S(2)}, u32[]{:S(2)}) collective-permute-start(bf16[128,1920]{1,0:T(8,128)(2,1)S(1)} %collective-permute-done.4), channel_id=1, source_target_pairs={{0,7},{1,0},{2,1},{3,2},{4,3},{5,4},{6,5},{7,6},{8,15},{9,8},{10,9... | collective-permute-start | bytes 1474568 | tf_op jit(solution)/shard_map/ppermute | solution.py:42
  70.5 3.2 %fusion.17 = bf16[1024,768]{1,0:T(8,128)(2,1)} fusion(bf16[1024,768]{1,0:T(8,128)(2,1)} %fusion.18, bf16[768,1408]{1,0:T(8,128)(2,1)} %bitcast.197, f32[1408]{0:T(1024)S(1)} %copy-done.16, f32[128]{0:T(128)S(1)} %add_rsqrt_fusion.8, f32[128]{0:T(128)S(1)} %broadcast_multiply_fusion.7, bf16[128,1920]{1,0:T(8,128)(2,1)S(1)} %collective-permute-done), kind=kOutput, calls=%fused_computation.42 | convolution fusion | flops 277823488 | bytes 2728960 | tf_op jit(solution)/shard_map/pi,oi->po/dot_general | solution.py:130
  76.5 3.4 %collective-permute-start.2 = (bf16[128,1920]{1,0:T(8,128)(2,1)S(1)}, bf16[128,1920]{1,0:T(8,128)(2,1)S(1)}, u32[]{:S(2)}, u32[]{:S(2)}) collective-permute-start(bf16[128,1920]{1,0:T(8,128)(2,1)S(1)} %collective-permute-done.1), channel_id=1, source_target_pairs={{0,1},{1,2},{2,3},{3,4},{4,5},{5,6},{6,7},{7,0},{8,9},{9,10},{10,1... | collective-permute-start | bytes 1474568 | tf_op jit(solution)/shard_map/ppermute | solution.py:39
  79.9 3.8 %collective-permute-start.6 = (bf16[128,1920]{1,0:T(8,128)(2,1)S(1)}, bf16[128,1920]{1,0:T(8,128)(2,1)S(1)}, u32[]{:S(2)}, u32[]{:S(2)}) collective-permute-start(bf16[128,1920]{1,0:T(8,128)(2,1)S(1)} %collective-permute-done.5), channel_id=1, source_target_pairs={{0,7},{1,0},{2,1},{3,2},{4,3},{5,4},{6,5},{7,6},{8,15},{9,8},{10,9... | collective-permute-start | bytes 1474568 | tf_op jit(solution)/shard_map/ppermute | solution.py:42
  86.1 2.4 collective-permute-done.2
  88.9 1.7 collective-permute-done.6
  90.7 3.6 %collective-permute-start.3 = (bf16[128,1920]{1,0:T(8,128)(2,1)S(1)}, bf16[128,1920]{1,0:T(8,128)(2,1)S(1)}, u32[]{:S(2)}, u32[]{:S(2)}) collective-permute-start(bf16[128,1920]{1,0:T(8,128)(2,1)S(1)} %collective-permute-done.2), channel_id=1, source_target_pairs={{0,1},{1,2},{2,3},{3,4},{4,5},{5,6},{6,7},{7,0},{8,9},{9,10},{10,1... | collective-permute-start | bytes 1474568 | tf_op jit(solution)/shard_map/ppermute | solution.py:39
  96.8 5.9 %collective-permute-done.3 = bf16[128,1920]{1,0:T(8,128)(2,1)S(1)} collective-permute-done((bf16[128,1920]{1,0:T(8,128)(2,1)S(1)}, bf16[128,1920]{1,0:T(8,128)(2,1)S(1)}, u32[]{:S(2)}, u32[]{:S(2)}) %collective-permute-start.3) | collective-permute-done | bytes 491552 | tf_op jit(solution)/shard_map/ppermute | solution.py:39
  107.3 2.1 copy.52
  109.4 1.9 gather_fusion.2
  111.4 1.8 fusion.70
  115.1 5.7 %fusion.19 = bf16[512,2,128]{0,2,1:T(8,128)(2,1)S(1)} fusion(bf16[1024,2,128]{0,2,1:T(8,128)(2,1)S(1)} %bitcast.209, f32[2,512]{1,0:T(2,128)S(1)} %fusion.165, f32[2,512,1024]{2,1,0:T(8,128)} %copy-done.2), kind=kOutput, calls=%fused_computation.45 | convolution fusion | flops 273811456 | bytes 4984832 | tf_op jit(solution)/shard_map/hsp,phd->shd/dot_general | solution.py:139
  121.9 7.2 %all-to-all-start.1 = ((bf16[8,64,176]{2,1,0:T(8,128)(2,1)}), bf16[8,64,176]{2,1,0:T(8,128)(2,1)S(1)}, u32[]{:S(2)}, u32[]{:S(2)}) async-start(bf16[8,64,176]{2,1,0:T(8,128)(2,1)} %reshape.527), calls=%async_computation.1 | async-start | bytes 524288 | tf_op jit(solution)/shard_map/all_to_all | solution.py:141
  129.1 1.6 fusion.131
  132.6 1.6 dynamic-slice_dynamic-update-slice_fusion.15
  134.2 1.6 dynamic-slice_dynamic-update-slice_fusion.14
  135.8 1.6 dynamic-slice_dynamic-update-slice_fusion.13
  137.3 1.6 dynamic-slice_dynamic-update-slice_fusion.12
  138.9 1.6 dynamic-slice_dynamic-update-slice_fusion.11
  140.5 1.6 dynamic-slice_dynamic-update-slice_fusion.10
  148.5 7.4 %fusion.5 = f32[4,128]{1,0:T(4,128)S(1)} fusion(f32[4,128]{1,0:T(4,128)S(1)} %get-tuple-element.24, bf16[8,128,4,128]{3,2,1,0:T(4,128)(2,1)S(1)} %reshape.511), kind=kLoop, calls=%fused_computation.15 | loop fusion | flops 2096640 | bytes 1052672 | tf_op jit(solution)/shard_map/reduce_sum | solution.py:17
  155.9 1.8 multiply_convert_fusion.1
  158.9 1.7 convolution_convert_fusion.2
  160.7 7.3 %all-to-all-start = ((bf16[8,64,1024]{2,1,0:T(8,128)(2,1)}), bf16[8,64,1024]{2,1,0:T(8,128)(2,1)S(1)}, u32[]{:S(2)}, u32[]{:S(2)}) async-start(bf16[8,64,1024]{2,1,0:T(8,128)(2,1)} %bitcast.206), calls=%async_computation | async-start | bytes 2097152 | tf_op jit(solution)/shard_map/all_to_all | solution.py:119
  168.0 1.8 slice_dynamic-update-slice_fusion.3
  169.8 1.8 slice_dynamic-update-slice_fusion.2
  173.1 3.1 gather_fusion.1
  176.6 6.1 %all-to-all-done = bf16[8,64,1024]{2,1,0:T(8,128)(2,1)S(1)} async-done(((bf16[8,64,1024]{2,1,0:T(8,128)(2,1)}), bf16[8,64,1024]{2,1,0:T(8,128)(2,1)S(1)}, u32[]{:S(2)}, u32[]{:S(2)}) %all-to-all-start) | async-done | bytes 1048608 | tf_op jit(solution)/shard_map/all_to_all | solution.py:119
  182.9 2.0 slice.146
  184.9 1.6 copy-done.1
  186.5 1.9 fusion.127
  188.4 21.5 %all-gather.5.cloned.1.call-done = bf16[8,256,8,128]{3,2,1,0:T(8,128)(2,1)} async-done(((bf16[8,4,8,128]{3,2,1,0:T(8,128)(2,1)}), bf16[8,256,8,128]{3,2,1,0:T(8,128)(2,1)}) %all-gather.5.cloned.1.call-update) | async-done | bytes 4194320 | tf_op jit(solution)/shard_map/all_gather | solution.py:107
  209.9 2.1 slice-done
  213.7 2.5 convolution_convert_fusion.11
  216.2 2.5 collective-permute-start.14
  218.7 4.6 %collective-permute-start.18 = (bf16[64,1152]{1,0:T(8,128)(2,1)S(1)}, bf16[64,1152]{1,0:T(8,128)(2,1)S(1)}, u32[]{:S(2)}, u32[]{:S(2)}) collective-permute-start(bf16[64,1152]{1,0:T(8,128)(2,1)S(1)} %fusion.126), channel_id=1, source_target_pairs={{0,7},{1,0},{2,1},{3,2},{4,3},{5,4},{6,5},{7,6},{8,15},{9,8},{10,9... | collective-permute-start | bytes 442376 | tf_op jit(solution)/shard_map/ppermute | solution.py:42
  223.3 2.0 collective-permute-done.14
  225.4 1.9 collective-permute-start.15
  227.3 5.3 %collective-permute-start.19 = (bf16[64,1152]{1,0:T(8,128)(2,1)S(1)}, bf16[64,1152]{1,0:T(8,128)(2,1)S(1)}, u32[]{:S(2)}, u32[]{:S(2)}) collective-permute-start(bf16[64,1152]{1,0:T(8,128)(2,1)S(1)} %collective-permute-done.18), channel_id=1, source_target_pairs={{0,7},{1,0},{2,1},{3,2},{4,3},{5,4},{6,5},{7,6},{8,15},{9,8},{10,9... | collective-permute-start | bytes 442376 | tf_op jit(solution)/shard_map/ppermute | solution.py:42
  233.7 1.9 collective-permute-start.16
  235.6 5.2 %collective-permute-start.20 = (bf16[64,1152]{1,0:T(8,128)(2,1)S(1)}, bf16[64,1152]{1,0:T(8,128)(2,1)S(1)}, u32[]{:S(2)}, u32[]{:S(2)}) collective-permute-start(bf16[64,1152]{1,0:T(8,128)(2,1)S(1)} %collective-permute-done.19), channel_id=1, source_target_pairs={{0,7},{1,0},{2,1},{3,2},{4,3},{5,4},{6,5},{7,6},{8,15},{9,8},{10,9... | collective-permute-start | bytes 442376 | tf_op jit(solution)/shard_map/ppermute | solution.py:42
  241.9 2.2 collective-permute-start.17
  244.1 6.0 %collective-permute-done.17 = bf16[64,1152]{1,0:T(8,128)(2,1)S(1)} collective-permute-done((bf16[64,1152]{1,0:T(8,128)(2,1)S(1)}, bf16[64,1152]{1,0:T(8,128)(2,1)S(1)}, u32[]{:S(2)}, u32[]{:S(2)}) %collective-permute-start.17) | collective-permute-done | bytes 147488 | tf_op jit(solution)/shard_map/ppermute | solution.py:39
  251.5 3.3 %convolution_convert_fusion.1 = bf16[1024,512]{1,0:T(8,128)(2,1)S(1)} fusion(bf16[512,1024]{1,0:T(8,128)(2,1)S(1)} %copy-done, f32[512,512]{1,0:T(8,128)} %get-tuple-element.28, bf16[512,1152]{1,0:T(8,128)(2,1)} %bitcast.214, f32[1024]{0:T(1024)S(1)} %copy-done.17, f32[512]{0:T(512)S(1)} %rsqrt_bitcast_fusion, f32[512]{0:T(512)S(1)} %get-tuple-element.23, ...), kind=kOutput, calls=%fused_computation.24 | convolution fusion | flops 1079508992 | bytes 5251072 | tf_op jit(solution)/shard_map/rd,rh->dh/dot_general | solution.py:168
  256.0 1.9 collective-permute-start.21
  257.9 3.0 collective-permute-done.21
  260.9 1.6 fusion.6
  262.6 19.4 %all_to_all.24 = bf16[1,8,4,32,512]{4,3,1,0,2:T(8,128)(2,1)S(1)} all-to-all(bf16[1,8,4,32,512]{4,3,1,0,2:T(8,128)(2,1)S(1)} %copy.51), channel_id=1, replica_groups=mesh['z'=8,'x'=4,'c'=2,'mp'=8] {'x'}, dimensions={2} | all-to-all | bytes 2097152 | tf_op jit(solution)/shard_map/all_to_all | solution.py:177
  282.9 4.8 %all-to-all-start.3 = ((bf16[8,32,512]{2,1,0:T(8,128)(2,1)}), bf16[8,32,512]{2,1,0:T(8,128)(2,1)S(1)}, u32[]{:S(2)}, u32[]{:S(2)}) async-start(bf16[8,32,512]{2,1,0:T(8,128)(2,1)} %reduce_sum.260), calls=%async_computation.3 | async-start | bytes 524288 | tf_op jit(solution)/shard_map/all_to_all | solution.py:179
  287.7 1.6 convert_reduce_fusion.11
  289.3 9.2 %all-to-all-done.3 = bf16[8,32,512]{2,1,0:T(8,128)(2,1)S(1)} async-done(((bf16[8,32,512]{2,1,0:T(8,128)(2,1)}), bf16[8,32,512]{2,1,0:T(8,128)(2,1)S(1)}, u32[]{:S(2)}, u32[]{:S(2)}) %all-to-all-start.3) | async-done | bytes 262176 | tf_op jit(solution)/shard_map/all_to_all | solution.py:179
  (184 shorter events, 46.8 us)
Async XLA Ops:
  7.2 151.8 %copy-start = (bf16[512,1024]{1,0:T(8,128)(2,1)S(1)}, bf16[512,1024]{1,0:T(8,128)(2,1)}, u32[]{:S(2)}) copy-start(bf16[512,1024]{1,0:T(8,128)(2,1)} %param.18) | copy-start | bytes 3145732
  7.2 34.0 %copy-start.14 = (s32[1,512]{1,0:T(1,128)S(1)}, s32[1,512]{1,0:T(1,128)}, u32[]{:S(2)}) copy-start(s32[1,512]{1,0:T(1,128)} %param.20) | copy-start | bytes 6148
  7.2 34.1 %copy-start.3 = (bf16[1,1024,128]{2,1,0:T(8,128)(2,1)S(1)}, bf16[1,1024,128]{2,1,0:T(8,128)(2,1)}, u32[]{:S(2)}) copy-start(bf16[1,1024,128]{2,1,0:T(8,128)(2,1)} %param.15) | copy-start | bytes 786436
  7.2 35.4 %copy-start.5 = (bf16[1,128,1408]{2,1,0:T(8,128)(2,1)S(1)}, bf16[1,128,1408]{2,1,0:T(8,128)(2,1)}, u32[]{:S(2)}) copy-start(bf16[1,128,1408]{2,1,0:T(8,128)(2,1)} %param.11) | copy-start | bytes 1081348
  7.2 175.6 %all-gather.3.cloned.1.call-start = ((), (), s32[]{:S(2)}) async-start(), calls=%async_computation.4 | async-start | bytes 3194880 | tf_op jit(solution)/shard_map/all_gather | solution.py:108
  9.5 19.6 %collective-permute-start.7 = (bf16[1,7,8,128]{3,2,1,0:T(8,128)(2,1)S(1)}, bf16[1,7,8,128]{3,2,1,0:T(8,128)(2,1)S(1)}, u32[]{:S(2)}, u32[]{:S(2)}) collective-permute-start(bf16[1,7,8,128]{3,2,1,0:T(8,128)(2,1)S(1)} %maximum_bitcast_fusion.1), channel_id=1, source_target_pairs={{0,1},{1,0},{2,3},{3,2},{4,5},{5,4},{6,7},{7,6},{8,9},{9,8},{10,11... | collective-permute-start | bytes 43016 | tf_op jit(solution)/shard_map/ppermute | solution.py:104
  12.1 21.6 %collective-permute-start.8 = (bf16[1,7,8,128]{3,2,1,0:T(8,128)(2,1)S(1)}, bf16[1,7,8,128]{3,2,1,0:T(8,128)(2,1)S(1)}, u32[]{:S(2)}, u32[]{:S(2)}) collective-permute-start(bf16[1,7,8,128]{3,2,1,0:T(8,128)(2,1)S(1)} %maximum_bitcast_fusion.1), channel_id=1, source_target_pairs={{0,2},{1,3},{2,0},{3,1},{4,6},{5,7},{6,4},{7,5},{8,10},{9,11},{10,... | collective-permute-start | bytes 43016 | tf_op jit(solution)/shard_map/ppermute | solution.py:104
  14.8 21.8 %collective-permute-start.9 = (bf16[1,7,8,128]{3,2,1,0:T(8,128)(2,1)S(1)}, bf16[1,7,8,128]{3,2,1,0:T(8,128)(2,1)S(1)}, u32[]{:S(2)}, u32[]{:S(2)}) collective-permute-start(bf16[1,7,8,128]{3,2,1,0:T(8,128)(2,1)S(1)} %maximum_bitcast_fusion.1), channel_id=1, source_target_pairs={{0,3},{1,2},{2,1},{3,0},{4,7},{5,6},{6,5},{7,4},{8,11},{9,10},{10,... | collective-permute-start | bytes 43016 | tf_op jit(solution)/shard_map/ppermute | solution.py:104
  19.6 17.0 %collective-permute-start.10 = (bf16[1,7,8,128]{3,2,1,0:T(8,128)(2,1)S(1)}, bf16[1,7,8,128]{3,2,1,0:T(8,128)(2,1)S(1)}, u32[]{:S(2)}, u32[]{:S(2)}) collective-permute-start(bf16[1,7,8,128]{3,2,1,0:T(8,128)(2,1)S(1)} %maximum_bitcast_fusion.1), channel_id=1, source_target_pairs={{0,4},{1,5},{2,6},{3,7},{4,0},{5,1},{6,2},{7,3},{8,12},{9,13},{10,... | collective-permute-start | bytes 43016 | tf_op jit(solution)/shard_map/ppermute | solution.py:104
  27.0 9.6 %collective-permute-start.11 = (bf16[1,7,8,128]{3,2,1,0:T(8,128)(2,1)S(1)}, bf16[1,7,8,128]{3,2,1,0:T(8,128)(2,1)S(1)}, u32[]{:S(2)}, u32[]{:S(2)}) collective-permute-start(bf16[1,7,8,128]{3,2,1,0:T(8,128)(2,1)S(1)} %maximum_bitcast_fusion.1), channel_id=1, source_target_pairs={{0,5},{1,4},{2,7},{3,6},{4,1},{5,0},{6,3},{7,2},{8,13},{9,12},{10,... | collective-permute-start | bytes 43016 | tf_op jit(solution)/shard_map/ppermute | solution.py:104
  29.1 7.7 %collective-permute-start.12 = (bf16[1,7,8,128]{3,2,1,0:T(8,128)(2,1)S(1)}, bf16[1,7,8,128]{3,2,1,0:T(8,128)(2,1)S(1)}, u32[]{:S(2)}, u32[]{:S(2)}) collective-permute-start(bf16[1,7,8,128]{3,2,1,0:T(8,128)(2,1)S(1)} %maximum_bitcast_fusion.1), channel_id=1, source_target_pairs={{0,6},{1,7},{2,4},{3,5},{4,2},{5,3},{6,0},{7,1},{8,14},{9,15},{10,... | collective-permute-start | bytes 43016 | tf_op jit(solution)/shard_map/ppermute | solution.py:104
  33.7 6.8 %collective-permute-start.13 = (bf16[1,7,8,128]{3,2,1,0:T(8,128)(2,1)S(1)}, bf16[1,7,8,128]{3,2,1,0:T(8,128)(2,1)S(1)}, u32[]{:S(2)}, u32[]{:S(2)}) collective-permute-start(bf16[1,7,8,128]{3,2,1,0:T(8,128)(2,1)S(1)} %maximum_bitcast_fusion.1), channel_id=1, source_target_pairs={{0,7},{1,6},{2,5},{3,4},{4,3},{5,2},{6,1},{7,0},{8,15},{9,14},{10,... | collective-permute-start | bytes 43016 | tf_op jit(solution)/shard_map/ppermute | solution.py:104
  41.2 168.7 %all-gather.5.cloned.1.call-start = ((), (), s32[]{:S(2)}) async-start(), calls=%async_computation.5 | async-start | bytes 4259840 | tf_op jit(solution)/shard_map/all_gather | solution.py:107
  46.1 15.9 %collective-permute-start = (bf16[128,1920]{1,0:T(8,128)(2,1)}, bf16[128,1920]{1,0:T(8,128)(2,1)S(1)}, u32[]{:S(2)}, u32[]{:S(2)}) collective-permute-start(bf16[128,1920]{1,0:T(8,128)(2,1)} %get-tuple-element.14), channel_id=1, source_target_pairs={{0,1},{1,2},{2,3},{3,4},{4,5},{5,6},{6,7},{7,0},{8,9},{9,10},{10,1... | collective-permute-start | bytes 1474568 | tf_op jit(solution)/shard_map/ppermute | solution.py:39
  50.4 12.1 %collective-permute-start.4 = (bf16[128,1920]{1,0:T(8,128)(2,1)}, bf16[128,1920]{1,0:T(8,128)(2,1)S(1)}, u32[]{:S(2)}, u32[]{:S(2)}) collective-permute-start(bf16[128,1920]{1,0:T(8,128)(2,1)} %get-tuple-element.14), channel_id=1, source_target_pairs={{0,7},{1,0},{2,1},{3,2},{4,3},{5,4},{6,5},{7,6},{8,15},{9,8},{10,9... | collective-permute-start | bytes 1474568 | tf_op jit(solution)/shard_map/ppermute | solution.py:42
  53.3 5.0 %copy-start.16 = (f32[1408]{0:T(1024)S(1)}, f32[1408]{0:T(1024)}, u32[]{:S(2)}) copy-start(f32[1408]{0:T(1024)} %param.12) | copy-start | bytes 16900
  62.6 12.0 %collective-permute-start.1 = (bf16[128,1920]{1,0:T(8,128)(2,1)S(1)}, bf16[128,1920]{1,0:T(8,128)(2,1)S(1)}, u32[]{:S(2)}, u32[]{:S(2)}) collective-permute-start(bf16[128,1920]{1,0:T(8,128)(2,1)S(1)} %collective-permute-done), channel_id=1, source_target_pairs={{0,1},{1,2},{2,3},{3,4},{4,5},{5,6},{6,7},{7,0},{8,9},{9,10},{10,1... | collective-permute-start | bytes 1474568 | tf_op jit(solution)/shard_map/ppermute | solution.py:39
  65.6 10.7 %collective-permute-start.5 = (bf16[128,1920]{1,0:T(8,128)(2,1)S(1)}, bf16[128,1920]{1,0:T(8,128)(2,1)S(1)}, u32[]{:S(2)}, u32[]{:S(2)}) collective-permute-start(bf16[128,1920]{1,0:T(8,128)(2,1)S(1)} %collective-permute-done.4), channel_id=1, source_target_pairs={{0,7},{1,0},{2,1},{3,2},{4,3},{5,4},{6,5},{7,6},{8,15},{9,8},{10,9... | collective-permute-start | bytes 1474568 | tf_op jit(solution)/shard_map/ppermute | solution.py:42
  70.5 14.0 %copy-start.10 = (bf16[3,2,128,1408]{3,2,1,0:T(8,128)(2,1)S(1)}, bf16[3,2,128,1408]{3,2,1,0:T(8,128)(2,1)}, u32[]{:S(2)}) copy-start(bf16[3,2,128,1408]{3,2,1,0:T(8,128)(2,1)} %pad.10) | copy-start | bytes 6488068
  73.7 10.8 %copy-start.11 = (bf16[1024,768]{1,0:T(8,128)(2,1)S(1)}, bf16[1024,768]{1,0:T(8,128)(2,1)}, u32[]{:S(2)}) copy-start(bf16[1024,768]{1,0:T(8,128)(2,1)} %fusion.17) | copy-start | bytes 4718596
  76.4 55.0 %copy-start.6 = (bf16[128,1920]{1,0:T(8,128)(2,1)}, bf16[128,1920]{1,0:T(8,128)(2,1)S(1)}, u32[]{:S(2)}) copy-start(bf16[128,1920]{1,0:T(8,128)(2,1)S(1)} %collective-permute-done.5) | copy-start | bytes 1474564
  76.5 12.0 %collective-permute-start.2 = (bf16[128,1920]{1,0:T(8,128)(2,1)S(1)}, bf16[128,1920]{1,0:T(8,128)(2,1)S(1)}, u32[]{:S(2)}, u32[]{:S(2)}) collective-permute-start(bf16[128,1920]{1,0:T(8,128)(2,1)S(1)} %collective-permute-done.1), channel_id=1, source_target_pairs={{0,1},{1,2},{2,3},{3,4},{4,5},{5,6},{6,7},{7,0},{8,9},{9,10},{10,1... | collective-permute-start | bytes 1474568 | tf_op jit(solution)/shard_map/ppermute | solution.py:39
  79.9 10.7 %collective-permute-start.6 = (bf16[128,1920]{1,0:T(8,128)(2,1)S(1)}, bf16[128,1920]{1,0:T(8,128)(2,1)S(1)}, u32[]{:S(2)}, u32[]{:S(2)}) collective-permute-start(bf16[128,1920]{1,0:T(8,128)(2,1)S(1)} %collective-permute-done.5), channel_id=1, source_target_pairs={{0,7},{1,0},{2,1},{3,2},{4,3},{5,4},{6,5},{7,6},{8,15},{9,8},{10,9... | collective-permute-start | bytes 1474568 | tf_op jit(solution)/shard_map/ppermute | solution.py:42
  90.6 40.1 %copy-start.8 = (bf16[128,1920]{1,0:T(8,128)(2,1)}, bf16[128,1920]{1,0:T(8,128)(2,1)S(1)}, u32[]{:S(2)}) copy-start(bf16[128,1920]{1,0:T(8,128)(2,1)S(1)} %collective-permute-done.6) | copy-start | bytes 1474564
  90.7 11.9 %collective-permute-start.3 = (bf16[128,1920]{1,0:T(8,128)(2,1)S(1)}, bf16[128,1920]{1,0:T(8,128)(2,1)S(1)}, u32[]{:S(2)}, u32[]{:S(2)}) collective-permute-start(bf16[128,1920]{1,0:T(8,128)(2,1)S(1)} %collective-permute-done.2), channel_id=1, source_target_pairs={{0,1},{1,2},{2,3},{3,4},{4,5},{5,6},{6,7},{7,0},{8,9},{9,10},{10,1... | collective-permute-start | bytes 1474568 | tf_op jit(solution)/shard_map/ppermute | solution.py:39
  102.7 2.0 copy-start.9
  113.1 1.9 copy-start.2
  113.1 1.9 copy-start.12
  121.9 38.8 %all-to-all-start.1 = ((bf16[8,64,176]{2,1,0:T(8,128)(2,1)}), bf16[8,64,176]{2,1,0:T(8,128)(2,1)S(1)}, u32[]{:S(2)}, u32[]{:S(2)}) async-start(bf16[8,64,176]{2,1,0:T(8,128)(2,1)} %reshape.527), calls=%async_computation.1 | async-start | bytes 524288 | tf_op jit(solution)/shard_map/all_to_all | solution.py:141
  146.5 9.4 %copy-start.15 = (bf16[1024,512]{1,0:T(8,128)(2,1)S(1)}, bf16[1024,512]{1,0:T(8,128)(2,1)}, u32[]{:S(2)}) copy-start(bf16[1024,512]{1,0:T(8,128)(2,1)} %param.17) | copy-start | bytes 3145732
  146.5 9.4 %copy-start.17 = (f32[1024]{0:T(1024)S(1)}, f32[1024]{0:T(1024)}, u32[]{:S(2)}) copy-start(f32[1024]{0:T(1024)} %param.16) | copy-start | bytes 12292
  147.2 10.5 %copy-start.4 = (bf16[8,128,4,128]{3,0,1,2:T(8,128)(2,1)}, bf16[8,128,4,128]{3,0,1,2:T(8,128)(2,1)S(1)}, u32[]{:S(2)}) copy-start(bf16[8,128,4,128]{3,0,1,2:T(8,128)(2,1)S(1)} %copy.42) | copy-start | bytes 3145732
  157.7 1.3 copy-start.18
  160.7 10.9 %copy-start.7 = (bf16[128,1920]{1,0:T(8,128)(2,1)S(1)}, bf16[128,1920]{1,0:T(8,128)(2,1)}, u32[]{:S(2)}) copy-start(bf16[128,1920]{1,0:T(8,128)(2,1)} %copy-done.6) | copy-start | bytes 1474564
  160.7 22.0 %all-to-all-start = ((bf16[8,64,1024]{2,1,0:T(8,128)(2,1)}), bf16[8,64,1024]{2,1,0:T(8,128)(2,1)S(1)}, u32[]{:S(2)}, u32[]{:S(2)}) async-start(bf16[8,64,1024]{2,1,0:T(8,128)(2,1)} %bitcast.206), calls=%async_computation | async-start | bytes 2097152 | tf_op jit(solution)/shard_map/all_to_all | solution.py:119
  184.9 1.6 copy-start.1
  209.9 2.1 slice-start
  216.2 9.1 %collective-permute-start.14 = (bf16[64,1152]{1,0:T(8,128)(2,1)S(1)}, bf16[64,1152]{1,0:T(8,128)(2,1)S(1)}, u32[]{:S(2)}, u32[]{:S(2)}) collective-permute-start(bf16[64,1152]{1,0:T(8,128)(2,1)S(1)} %fusion.126), channel_id=1, source_target_pairs={{0,1},{1,2},{2,3},{3,4},{4,5},{5,6},{6,7},{7,0},{8,9},{9,10},{10,1... | collective-permute-start | bytes 442376 | tf_op jit(solution)/shard_map/ppermute | solution.py:39
  218.7 8.6 %collective-permute-start.18 = (bf16[64,1152]{1,0:T(8,128)(2,1)S(1)}, bf16[64,1152]{1,0:T(8,128)(2,1)S(1)}, u32[]{:S(2)}, u32[]{:S(2)}) collective-permute-start(bf16[64,1152]{1,0:T(8,128)(2,1)S(1)} %fusion.126), channel_id=1, source_target_pairs={{0,7},{1,0},{2,1},{3,2},{4,3},{5,4},{6,5},{7,6},{8,15},{9,8},{10,9... | collective-permute-start | bytes 442376 | tf_op jit(solution)/shard_map/ppermute | solution.py:42
  225.4 8.3 %collective-permute-start.15 = (bf16[64,1152]{1,0:T(8,128)(2,1)S(1)}, bf16[64,1152]{1,0:T(8,128)(2,1)S(1)}, u32[]{:S(2)}, u32[]{:S(2)}) collective-permute-start(bf16[64,1152]{1,0:T(8,128)(2,1)S(1)} %collective-permute-done.14), channel_id=1, source_target_pairs={{0,1},{1,2},{2,3},{3,4},{4,5},{5,6},{6,7},{7,0},{8,9},{9,10},{10,1... | collective-permute-start | bytes 442376 | tf_op jit(solution)/shard_map/ppermute | solution.py:39
  227.3 23.2 %copy-start.19 = (bf16[512,512]{1,0:T(8,128)(2,1)S(1)}, bf16[512,512]{1,0:T(8,128)(2,1)}, u32[]{:S(2)}) copy-start(bf16[512,512]{1,0:T(8,128)(2,1)} %copy-done.18) | copy-start | bytes 1572868
  227.3 8.3 %collective-permute-start.19 = (bf16[64,1152]{1,0:T(8,128)(2,1)S(1)}, bf16[64,1152]{1,0:T(8,128)(2,1)S(1)}, u32[]{:S(2)}, u32[]{:S(2)}) collective-permute-start(bf16[64,1152]{1,0:T(8,128)(2,1)S(1)} %collective-permute-done.18), channel_id=1, source_target_pairs={{0,7},{1,0},{2,1},{3,2},{4,3},{5,4},{6,5},{7,6},{8,15},{9,8},{10,9... | collective-permute-start | bytes 442376 | tf_op jit(solution)/shard_map/ppermute | solution.py:42
  233.7 8.2 %collective-permute-start.16 = (bf16[64,1152]{1,0:T(8,128)(2,1)S(1)}, bf16[64,1152]{1,0:T(8,128)(2,1)S(1)}, u32[]{:S(2)}, u32[]{:S(2)}) collective-permute-start(bf16[64,1152]{1,0:T(8,128)(2,1)S(1)} %collective-permute-done.15), channel_id=1, source_target_pairs={{0,1},{1,2},{2,3},{3,4},{4,5},{5,6},{6,7},{7,0},{8,9},{9,10},{10,1... | collective-permute-start | bytes 442376 | tf_op jit(solution)/shard_map/ppermute | solution.py:39
  235.6 14.5 %collective-permute-start.20 = (bf16[64,1152]{1,0:T(8,128)(2,1)S(1)}, bf16[64,1152]{1,0:T(8,128)(2,1)S(1)}, u32[]{:S(2)}, u32[]{:S(2)}) collective-permute-start(bf16[64,1152]{1,0:T(8,128)(2,1)S(1)} %collective-permute-done.19), channel_id=1, source_target_pairs={{0,7},{1,0},{2,1},{3,2},{4,3},{5,4},{6,5},{7,6},{8,15},{9,8},{10,9... | collective-permute-start | bytes 442376 | tf_op jit(solution)/shard_map/ppermute | solution.py:42
  241.9 8.2 %collective-permute-start.17 = (bf16[64,1152]{1,0:T(8,128)(2,1)S(1)}, bf16[64,1152]{1,0:T(8,128)(2,1)S(1)}, u32[]{:S(2)}, u32[]{:S(2)}) collective-permute-start(bf16[64,1152]{1,0:T(8,128)(2,1)S(1)} %collective-permute-done.16), channel_id=1, source_target_pairs={{0,1},{1,2},{2,3},{3,4},{4,5},{5,6},{6,7},{7,0},{8,9},{9,10},{10,1... | collective-permute-start | bytes 442376 | tf_op jit(solution)/shard_map/ppermute | solution.py:39
  250.5 1.1 copy-start.13
  256.0 4.9 %collective-permute-start.21 = (bf16[32,32,512]{2,1,0:T(8,128)(2,1)}, bf16[32,32,512]{2,1,0:T(8,128)(2,1)}, u32[]{:S(2)}, u32[]{:S(2)}) collective-permute-start(bf16[32,32,512]{2,1,0:T(8,128)(2,1)} %fusion.25), channel_id=1, source_target_pairs={{0,8},{8,0},{1,9},{9,1},{2,10},{10,2},{3,11},{11,3},{4,12},{12,4},... | collective-permute-start | bytes 3145736 | tf_op jit(solution)/shard_map/ppermute | solution.py:174
  282.9 15.6 %all-to-all-start.3 = ((bf16[8,32,512]{2,1,0:T(8,128)(2,1)}), bf16[8,32,512]{2,1,0:T(8,128)(2,1)S(1)}, u32[]{:S(2)}, u32[]{:S(2)}) async-start(bf16[8,32,512]{2,1,0:T(8,128)(2,1)} %reduce_sum.260), calls=%async_computation.3 | async-start | bytes 524288 | tf_op jit(solution)/shard_map/all_to_all | solution.py:179
Sparse Core Ops, SparseCore 0:
  41.3 83.5 all-gather.2
  128.1 81.7 all-gather.4
